TPU v7x, 32 devices: a whole 2x2x4 slice. The times are simulated.
32 devices in a mesh: traj: 8 (over z, y), seg: 4 (over x, core).
Axes of the slice: x: 2, y: 2, z: 4, core: 2. Of those that a mesh axis runs over, the one named last changes fastest.
Arguments:
- coords: float32 [8, 512, 3, 512], P('traj', 'seg')
- pairs: int32 [2, 1024], replicated, may hold values from 0 to 511, as said below
- lengths: int32 [8], P('traj'), may hold values from 1 to 512, 3072 in all
Outputs:
- projected: float32 [8, 512, 128], P('traj', 'seg')
Inputs may be any that keep to these rules, and one draw needn't show every extreme that they name: `pairs`: atom indices; the two atoms of a contact differ. `lengths`: each trajectory's recorded frames fill its first slots.
All inputs are finite; a program needn't handle non-finite values. No bound on the sum of `lengths` on one device may be relied on, other than what follows from the above.
Results may differ from a plain program's by a relative error of at most 0.0003.
Values sent between devices are 32-bit elements; how exact they have to be, the bound alone decides.
A program may use at most 128 MiB of HBM per device.

v0:
```python
import jax
import jax.numpy as jnp
from jax import lax
from jax.experimental import pallas as pl
from jax.experimental.pallas import tpu as pltpu
from jax.sharding import PartitionSpec as P

K = 128
LAG = 10
ITERS = 3
BLOCK = 128
GROUP = 4


exact_mode = lax.Precision.HIGHEST
soft_square = 0.1
ridge_term = 0.01
spectral_shift = 2.0


def exact_dot(left, right, left_axis=1, right_axis=0):
    return lax.dot_general(
        left,
        right,
        (((left_axis,), (right_axis,)), ((), ())),
        precision=exact_mode,
        preferred_element_type=jnp.float32,
    )


def split3(x):
    high = x.astype(jnp.bfloat16)
    rest = x - high.astype(jnp.float32)
    middle = rest.astype(jnp.bfloat16)
    low = (rest - middle.astype(jnp.float32)).astype(jnp.bfloat16)
    return high, middle, low


def inverse_factor(matrix):
    size = matrix.shape[0]
    lane = lax.broadcasted_iota(jnp.int32, (8, size), 1)
    sub = lax.broadcasted_iota(jnp.int32, (8, size), 0)
    rest = matrix.reshape(size // 8, 8, size)
    finished = []
    for start in range(0, size, GROUP):
        top = start % 8
        head = rest[0]
        pivots = [
            [
                jnp.broadcast_to(head[top + a : top + a + 1, start + b : start + b + 1], (8, size))
                if b >= a
                else None
                for b in range(GROUP)
            ]
            for a in range(GROUP)
        ]
        columns = [
            jnp.broadcast_to(rest[:, :, start + a : start + a + 1], rest.shape)
            for a in range(GROUP)
        ]
        rows, inverses = [], []
        for a in range(GROUP):
            row = jnp.broadcast_to(head[top + a : top + a + 1, :], (8, size))
            row = jnp.where((lane >= start) & (lane < start + GROUP), 0.0, row)
            for b in range(a):
                row = row - (pivots[b][a] * inverses[b]) * rows[b]
            inverse = 1.0 / pivots[a][a]
            for b in range(a + 1, GROUP):
                scale = pivots[a][b] * inverse
                for c in range(b, GROUP):
                    pivots[b][c] = pivots[b][c] - scale * pivots[a][c]
            rows.append(jnp.where(lane == start + a, 1.0, row))
            inverses.append(inverse)
        scaled = []
        for a in range(GROUP):
            column = columns[a]
            for b in range(a):
                column = column - scaled[b] * pivots[b][a][None]
            scaled.append(column * inverses[a][None])
        cleared = jnp.where(((lane >= start) & (lane < start + GROUP))[None], 0.0, rest)
        update = scaled[0] * rows[0][None]
        for a in range(1, GROUP):
            update = update + scaled[a] * rows[a][None]
        fresh = cleared - update
        head = jnp.where(sub >= top + GROUP, fresh[0], head)
        for a in range(GROUP):
            head = jnp.where(sub == top + a, rows[a] * jnp.sqrt(inverses[a]), head)
        if top + GROUP == 8:
            finished.append(head)
            rest = fresh[1:] if start + GROUP < size else None
        else:
            rest = jnp.concatenate([head[None], fresh[1:]], axis=0) if len(fresh) > 1 else head[None]
    out = jnp.concatenate(finished, axis=0)
    row_index = lax.broadcasted_iota(jnp.int32, (size, size), 0)
    lane_index = lax.broadcasted_iota(jnp.int32, (size, size), 1)
    return jnp.where(lane_index <= row_index, out, 0.0)


def fold(matrix):
    blocks = matrix.shape[0] // BLOCK
    bands = []
    for i in range(blocks // 2):
        j = blocks - 1 - i
        low = matrix[i * BLOCK : (i + 1) * BLOCK, : (i + 1) * BLOCK]
        high = matrix[j * BLOCK : (j + 1) * BLOCK, : (j + 1) * BLOCK]
        bands.append(jnp.concatenate([low, high], axis=1))
    return jnp.concatenate(bands, axis=0)


def folded_blocks(blocks):
    for i in range(blocks):
        band, begin = (i, 0) if i < blocks // 2 else (blocks - 1 - i, blocks - i)
        for j in range(i + 1):
            yield i, j, band, begin + j


def block_of(i):
    return slice(i * BLOCK, (i + 1) * BLOCK)


def inverse_kernel(tile, folded_ref, left_ref, right_ref, scale_ref, out_ref, first_ref, image_ref, wide):
    size = out_ref.shape[0]
    scale = scale_ref[0, 0]
    row_index = lax.broadcasted_iota(jnp.int32, (BLOCK, BLOCK), 0)
    lane_index = lax.broadcasted_iota(jnp.int32, (BLOCK, BLOCK), 1)
    ridge = jnp.where(row_index == lane_index, ridge_term, 0.0)
    for i, j, band, place in folded_blocks(size // BLOCK):
        between = exact_dot(left_ref[:, block_of(i)], right_ref[:, block_of(j)], 0, 0)
        block = (folded_ref[block_of(band), block_of(place)] + between) * scale
        if i == j:
            out_ref[block_of(i), block_of(i)] = block + ridge
        else:
            out_ref[block_of(i), block_of(j)] = block
            out_ref[block_of(j), block_of(i)] = block.T

    @pl.loop(0, size // BLOCK)
    def _(k):
        here = pl.ds(pl.multiple_of(k * BLOCK, BLOCK), BLOCK)
        factor = inverse_factor(out_ref[here, here])

        @pl.when(k == 0)
        def _():
            first_ref[...] = factor
            image_ref[...] = exact_dot(out_ref[:, :BLOCK], factor, 1, 1)

        pivot = exact_dot(factor, factor, 0, 0)
        row = exact_dot(pivot, out_ref[here, :])
        high, middle, low = split3(row)
        for place, piece in enumerate((high, middle, high, middle, low, high)):
            wide[place * BLOCK : (place + 1) * BLOCK, :] = piece

        @pl.loop(0, size // tile)
        def _(i):
            span = pl.ds(pl.multiple_of(i * tile, tile), tile)
            column = out_ref[span, here]
            h, m, l = split3(column)
            long = jnp.concatenate([h, h, m, m, h, l], axis=1)
            out_ref[span, :] -= jnp.dot(long, wide[...], preferred_element_type=jnp.float32)
            out_ref[span, here] = exact_dot(column, pivot)

        out_ref[here, :] = row
        out_ref[here, here] = -pivot


def negative_inverse(folded, left, right, scale):
    size = left.shape[1]
    vmem, smem = pl.BlockSpec(memory_space=pltpu.VMEM), pl.BlockSpec(memory_space=pltpu.SMEM)
    return pl.pallas_call(
        lambda *refs: inverse_kernel(min(256, size), *refs),
        out_shape=(
            jax.ShapeDtypeStruct((size, size), jnp.float32),
            jax.ShapeDtypeStruct((BLOCK, BLOCK), jnp.float32),
            jax.ShapeDtypeStruct((size, BLOCK), jnp.float32),
        ),
        in_specs=[vmem, vmem, vmem, smem],
        out_specs=(vmem, vmem, vmem),
        scratch_shapes=[pltpu.VMEM((6 * BLOCK, size), jnp.bfloat16)],
        compiler_params=pltpu.CompilerParams(vmem_limit_bytes=40 * 1024 * 1024),
        cost_estimate=pl.CostEstimate(
            flops=120 * size * size * size, bytes_accessed=8 * size * size, transcendentals=0
        ),
        name="negative_inverse",
    )(folded, left, right, scale)


def sweep_kernel(
    tile, folded_ref, left_ref, right_ref, scale_ref, inverse_ref, first_ref, image_ref, shifted_ref,
    out_ref, lag_wide, inverse_wide, vector_wide, vector_tall, moved, basis, image,
):
    size = inverse_ref.shape[0]
    scale = scale_ref[0, 0]

    def put(wide, rows, columns, block):
        for place, piece in enumerate(split3(block)):
            wide[place, rows, columns] = piece

    for i, j, band, place in folded_blocks(size // BLOCK):
        between = exact_dot(left_ref[:, block_of(i)], right_ref[:, block_of(j)], 0, 0)
        block = (folded_ref[block_of(band), block_of(place)] + between) * scale
        put(lag_wide, block_of(i), block_of(j), block)
        if i != j:
            put(lag_wide, block_of(j), block_of(i), block.T)

    @pl.loop(0, size // BLOCK)
    def _(i):
        span = pl.ds(pl.multiple_of(i * BLOCK, BLOCK), BLOCK)
        put(inverse_wide, span, slice(None), inverse_ref[span, :])

    def multiply(wide, vector, sink):
        depth = vector.shape[0]
        high, middle, low = split3(vector)
        vector_wide[:depth, :] = jnp.concatenate([high, middle], axis=1)
        vector_tall[:depth, :] = low
        vector_tall[depth : 2 * depth, :] = high

        @pl.loop(0, size // tile)
        def _(i):
            span = pl.ds(pl.multiple_of(i * tile, tile), tile)
            pair = vector_wide[:depth, :]
            main = jnp.dot(wide[0, span, :depth], pair, preferred_element_type=jnp.float32)
            side = jnp.dot(wide[1, span, :depth], pair, preferred_element_type=jnp.float32)
            ends = jnp.concatenate([wide[0, span, :depth], wide[2, span, :depth]], axis=1)
            last = jnp.dot(ends, vector_tall[: 2 * depth, :], preferred_element_type=jnp.float32)
            both = main + side
            sink(span, both[:, :K] + (both[:, K:] + last))

    def keep_moved(span, value):
        moved[span, :] = value

    def step_basis(span, value):
        basis[span, :] = spectral_shift * basis[span, :] - value

    seed = first_ref[...].T
    basis[...] = jnp.zeros_like(basis)
    basis[:K, :] = seed
    image[...] = image_ref[...]
    for sweep in range(ITERS):
        multiply(lag_wide, seed if sweep == 0 else basis[...], keep_moved)
        image[...] = spectral_shift * image[...] + moved[...]
        multiply(inverse_wide, moved[...], step_basis)
    factor = inverse_factor(exact_dot(basis[...], image[...], 0, 0))
    out_ref[...] = exact_dot(exact_dot(shifted_ref[...], basis[...]), factor, 1, 1)


def sweeps(folded, left, right, scale, inverse, first, image, shifted):
    size = left.shape[1]
    vmem, smem = pl.BlockSpec(memory_space=pltpu.VMEM), pl.BlockSpec(memory_space=pltpu.SMEM)
    return pl.pallas_call(
        lambda *refs: sweep_kernel(min(256, size), *refs),
        out_shape=jax.ShapeDtypeStruct((shifted.shape[0], K), jnp.float32),
        in_specs=[vmem, vmem, vmem, smem, vmem, vmem, vmem, vmem],
        out_specs=vmem,
        scratch_shapes=[
            pltpu.VMEM((3, size, size), jnp.bfloat16),
            pltpu.VMEM((3, size, size), jnp.bfloat16),
            pltpu.VMEM((size, 2 * K), jnp.bfloat16),
            pltpu.VMEM((2 * size, K), jnp.bfloat16),
            pltpu.VMEM((size, K), jnp.float32),
            pltpu.VMEM((size, K), jnp.float32),
            pltpu.VMEM((size, K), jnp.float32),
        ],
        compiler_params=pltpu.CompilerParams(vmem_limit_bytes=48 * 1024 * 1024),
        name="sweeps",
    )(folded, left, right, scale, inverse, first, image, shifted)


def featurize(frames, selection):
    frame_rows, parts, atoms = frames.shape
    offset = exact_dot(jnp.swapaxes(frames, 0, 1).reshape(parts * frame_rows, atoms), selection)
    offset = offset.reshape(parts, frame_rows, -1)
    return jnp.sqrt(jnp.sum(offset * offset, axis=0) + soft_square)


def on_device(coords, pairs, lengths):
    frames = coords[0]
    frame_rows, _, atoms = frames.shape
    feature_count = pairs.shape[1]
    trajs, segs = lax.axis_size("traj"), lax.axis_size("seg")
    devices = trajs * segs
    traj, seg = lax.axis_index("traj"), lax.axis_index("seg")
    me = traj * segs + seg
    length = lengths[0]

    arriving = lax.ppermute(frames[:LAG], "seg", [(i + 1, i) for i in range(segs - 1)])
    atom = jnp.arange(atoms, dtype=jnp.int32)[:, None]
    selection = (atom == pairs[0][None]).astype(jnp.float32) - (atom == pairs[1][None]).astype(
        jnp.float32
    )
    features = featurize(frames, selection)
    lagged = jnp.concatenate([features[LAG:], featurize(arriving, selection)], axis=0)

    frame_index = seg * frame_rows + jnp.arange(frame_rows, dtype=jnp.int32)
    is_valid = (frame_index < length).astype(jnp.float32)[:, None]
    paired = (frame_index + LAG < length).astype(jnp.float32)[:, None]
    count_all = jnp.maximum(jnp.sum(is_valid), 1.0)
    count_pair = jnp.maximum(jnp.sum(paired), 1.0)
    own_all = jnp.sum(features * is_valid, axis=0) / count_all
    own_lead = jnp.sum(features * paired, axis=0) / count_pair
    own_ahead = jnp.sum(lagged * paired, axis=0) / count_pair
    centered = (features - own_all) * is_valid
    lead_rows = (features - own_lead) * paired
    ahead_rows = (lagged - own_ahead) * paired
    gram_zero = exact_dot(centered, centered, 0, 0)
    gram_lag = exact_dot(
        jnp.concatenate([lead_rows, ahead_rows], axis=0),
        jnp.concatenate([ahead_rows, lead_rows], axis=0),
        0,
        0,
    )

    mine = (jnp.arange(devices) == me)[:, None]
    slot_length = jnp.where(
        (jnp.arange(trajs) == traj) & (seg == 0), length.astype(jnp.float32), 0.0
    )
    slot_length = jnp.pad(slot_length[None], ((0, 7), (0, feature_count - trajs)))

    def load_of(gram, slots):
        folded = fold(gram)
        rows = folded.shape[0]
        slots = jnp.concatenate(slots, axis=0)
        wide = -(-slots.size // (rows * BLOCK)) * BLOCK
        taken = wide * rows // feature_count
        slots = jnp.pad(slots, ((0, taken - slots.shape[0]), (0, 0)))
        return jnp.concatenate([folded, slots.reshape(rows, wide)], axis=1)

    def unload(total):
        wide = feature_count + BLOCK
        return total[:, :wide], total[:, wide:].reshape(-1, feature_count)

    first_load = load_of(gram_zero, [jnp.where(mine, own_all[None], 0.0), slot_length])
    first_total = lax.psum(first_load, ("traj", "seg"))
    second_load = load_of(
        gram_lag, [jnp.where(mine, own_lead[None], 0.0), jnp.where(mine, own_ahead[None], 0.0)]
    )
    second_load, first_total = lax.optimization_barrier((second_load, first_total))
    second_total = lax.psum(second_load, ("traj", "seg"))

    folded_zero, slots = unload(first_total)
    all_lengths = slots[devices, :trajs]
    begins = jnp.arange(segs, dtype=jnp.float32)[None] * frame_rows
    counts = jnp.clip(all_lengths[:, None] - begins, 0.0, frame_rows).reshape(devices, 1)
    pair_counts = jnp.clip(all_lengths[:, None] - LAG - begins, 0.0, frame_rows).reshape(devices, 1)
    frames_total, pairs_total = jnp.sum(counts), jnp.sum(pair_counts)
    device_all = slots[:devices]
    mean_all = jnp.sum(device_all * counts, axis=0) / frames_total
    spread_all = device_all - mean_all
    inverse, first_factor, image = negative_inverse(
        folded_zero, spread_all * counts, spread_all, (1.0 / frames_total).reshape(1, 1)
    )

    folded_lag, slots = unload(second_total)
    device_lead, device_ahead = slots[:devices], slots[devices : 2 * devices]
    spread_lead = device_lead - jnp.sum(device_lead * pair_counts, axis=0) / pairs_total
    spread_ahead = device_ahead - jnp.sum(device_ahead * pair_counts, axis=0) / pairs_total
    shifted = (features - mean_all) * is_valid
    projected = sweeps(
        folded_lag,
        jnp.concatenate([spread_lead * pair_counts, spread_ahead * pair_counts], axis=0),
        jnp.concatenate([spread_ahead, spread_lead], axis=0),
        (0.5 / pairs_total).reshape(1, 1),
        inverse,
        first_factor,
        image,
        shifted,
    )
    return projected[None]


def solution(mesh):
    return jax.shard_map(
        on_device,
        mesh=mesh,
        in_specs=(P("traj", "seg", None, None), P(), P("traj")),
        out_specs=P("traj", "seg", None),
        check_vma=False,
    )
```

profile of v0, /device:TPU:9, one launch (start us, length us, event | category | flops | bytes accessed | tf_op | source)
XLA Modules:
  0.0 347.0 jit_solution(17414306224956879)
XLA Ops:
  6.5 0.9 slice_bitcast_fusion
  7.4 2.6 collective-permute-start
  10.0 0.8 fusion.27
  10.8 4.3 %fusion.2 = f32[1024,384]{0,1:T(8,128)S(1)} fusion(f32[384,512]{1,0:T(8,128)} %bitcast.29, s32[1024]{0:T(1024)S(1)} %bitcast.32, s32[1024]{0:T(1024)S(1)} %bitcast.30), kind=kOutput, calls=%fused_computation.7 | convolution fusion | flops 2418933760 | bytes 2367488 | tf_op jit(solution)/shard_map/dot_general | solution.py:22
  16.1 0.7 fusion.24
  18.1 1.8 fusion.4
  20.0 0.3 multiply_reduce_fusion
  20.6 3.9 %fusion.16 = f32[1024,1024]{1,0:T(8,128)S(1)} fusion(f32[1024]{0:T(1024)S(1)} %broadcast_divide_fusion.3, f32[128]{0:T(128)S(1)} %get-tuple-element.29, f32[128,1024]{1,0:T(8,128)S(1)} %reduce_sum.108), kind=kOutput, calls=%fused_computation.23 | convolution fusion | flops 1611005952 | bytes 4723200 | tf_op jit(solution)/shard_map/dot_general | solution.py:22
  24.7 0.7 slice.141
  25.4 0.7 slice.139
  26.0 0.6 slice.137
  26.7 0.8 broadcast_select_fusion
  27.6 2.7 pad_maximum_fusion.1
  30.6 0.6 copy-done.3
  31.4 3.7 %fusion.5 = f32[1024,1024]{1,0:T(8,128)S(1)} fusion(f32[128,1024]{1,0:T(8,128)S(1)} %get-tuple-element.44, f32[128,1024]{1,0:T(8,128)S(1)} %get-tuple-element.43), kind=kOutput, calls=%fused_computation.10 | convolution fusion | flops 3221749760 | bytes 5242880 | tf_op jit(solution)/shard_map/dot_general | solution.py:22
  35.3 0.6 copy-done.4
  36.1 1.7 pad_maximum_fusion
  37.8 126.9 %all-reduce.5.cloned.1.call-done = f32[512,1280]{1,0:T(8,128)} async-done(((f32[512,1280]{1,0:T(8,128)}), f32[512,1280]{1,0:T(8,128)}) %all-reduce.5.cloned.1.call-update) | async-done | bytes 2621456 | tf_op jit(solution)/shard_map/psum | solution.py:331
  164.7 1.0 slice.121
  165.8 0.9 slice.126
  166.7 1.8 slice.125.refs_0_
  168.5 0.7 fusion.22
  170.1 0.7 broadcast_divide_fusion
  170.9 79.2 %negative_inverse.1 = (f32[1024,1024]{1,0:T(8,128)S(1)}, f32[128,128]{1,0:T(8,128)S(1)}, f32[1024,128]{1,0:T(8,128)S(1)}) custom-call(f32[512,1152]{1,0:T(8,128)S(1)} %slice.125.refs_0_, f32[32,1024]{1,0:T(8,128)S(1)} %get-tuple-element.22.refs_1_, f32[32,1024]{1,0:T(8,128)S(1)} %get-tuple-element.23.refs_2_, f32[1,1]{1,0:T(1,128)} %bitcast.13.refs_3_), custom_call_target="tpu_custom_call" | custom-call | flops 128849018880 | bytes 8388608 | tf_op jit(solution)/shard_map/negative_inverse/pallas_call | solution.py:168
  250.1 1.9 copy-done
  252.7 1.2 subtract_multiply_fusion.refs_7_
  253.9 51.9 %all-reduce.7.cloned.1.call-done = f32[512,1280]{1,0:T(8,128)} async-done(((f32[512,1280]{1,0:T(8,128)}), f32[512,1280]{1,0:T(8,128)}) %all-reduce.7.cloned.1.call-update) | async-done | bytes 2621456 | tf_op jit(solution)/shard_map/psum | solution.py:336
  305.8 1.0 fusion.26
  307.0 0.5 broadcast_divide_fusion.1
  307.5 0.5 broadcast_divide_fusion.2
  308.2 1.8 slice.145.refs_0_
  310.1 30.1 %sweeps.1 = f32[128,128]{1,0:T(8,128)} custom-call(f32[512,1152]{1,0:T(8,128)S(1)} %slice.145.refs_0_, f32[64,1024]{1,0:T(8,128)S(1)} %pad_maximum_fusion.4.refs_1_, f32[64,1024]{1,0:T(8,128)S(1)} %pad_maximum_fusion.5.refs_2_, f32[1,1]{1,0:T(1,128)} %bitcast.12.refs_3_, f32[1024,1024]{1,0:T(8,128)} %copy-done, f32[128,128]{1,0:T(8,128)S(1)} %get-tuple-element.13.refs_5_, ...), custom_call_target="tpu_custom_call" | custom-call | tf_op jit(solution)/shard_map/sweeps/pallas_call | solution.py:248
  (60 shorter events, 2.5 us)
Async XLA Ops:
  6.5 158.2 %all-reduce.5.cloned.1.call-start = ((), (), s32[]{:S(2)}) async-start(), calls=%async_computation | async-start | bytes 5242880 | tf_op jit(solution)/shard_map/psum | solution.py:331
  7.4 10.7 %collective-permute-start = (f32[10,3,512]{2,0,1:T(8,128)S(1)}, f32[10,3,512]{2,0,1:T(8,128)S(1)}, u32[]{:S(2)}, u32[]{:S(2)}) collective-permute-start(f32[10,3,512]{2,0,1:T(8,128)S(1)} %slice_bitcast_fusion), channel_id=1, source_target_pairs={{1,0},{2,1},{3,2},{5,4},{6,5},{7,6},{9,8},{10,9},{11,10},{13,12},{... | collective-permute-start | bytes 184328 | tf_op jit(solution)/shard_map/ppermute | solution.py:284
  15.3 15.3 %copy-start.1 = (f32[128,1024]{1,0:T(8,128)}, f32[128,1024]{1,0:T(8,128)S(1)}, u32[]{:S(2)}) copy-start(f32[128,1024]{1,0:T(8,128)S(1)} %reduce_sum.108) | copy-start | bytes 1572868
  20.0 0.6 copy-start.2
  30.3 0.8 copy-start.3
  30.3 275.5 %all-reduce.7.cloned.1.call-start = ((), (), s32[]{:S(2)}) async-start(), calls=%async_computation.1 | async-start | bytes 5242880 | tf_op jit(solution)/shard_map/psum | solution.py:336
  35.1 0.9 copy-start.4
  35.1 1.0 copy-start.5
  250.1 1.9 copy-start
Sparse Core Ops, SparseCore 0:
  30.4 134.2 all-reduce.4
  171.1 134.6 all-reduce.6
where the time goes:
time: 352 us; the launch traced here: 347 us
  waiting for transfers between devices  179 us (51%)
  Pallas kernels  109 us (31%)
  between operations  17.1 us (5%)
  local copies, waits for them, and re-layouts  14.4 us (4%)
  matrix products  13.6 us (4%)
  other arithmetic  10.9 us (3%)
    psum x1, waiting for transfers between devices, on_device(): first_total = lax.psum(first_load, ('traj', 'seg'))  127 us
    pallas_call x1, Pallas kernels, negative_inverse(): pl.pallas_call(lambda *refs: inverse_kernel(min(256, size), *refs), out_s...  79.2 us
    psum x1, waiting for transfers between devices, on_device(): second_total = lax.psum(second_load, ('traj', 'seg'))  51.9 us
    pallas_call x1, Pallas kernels, sweeps(): pl.pallas_call(lambda *refs: sweep_kernel(min(256, size), *refs), out_sha...  30.1 us
    dot_general x4, matrix products, exact_dot(): lax.dot_general(left, right, (((left_axis,), (right_axis,)), ((), ())), p...  13.6 us
  transfers between devices with their start and end apart: 3, of which 2 were waited for; matrix products, arithmetic and copies ran while one was open for 4% of the time, Pallas kernels for 23%

commit v1 on v0

--- a/solution.py
+++ b/solution.py
@@ -98,20 +98,15 @@
 
 def fold(matrix):
     blocks = matrix.shape[0] // BLOCK
-    bands = []
-    for i in range(blocks // 2):
-        j = blocks - 1 - i
-        low = matrix[i * BLOCK : (i + 1) * BLOCK, : (i + 1) * BLOCK]
-        high = matrix[j * BLOCK : (j + 1) * BLOCK, : (j + 1) * BLOCK]
-        bands.append(jnp.concatenate([low, high], axis=1))
-    return jnp.concatenate(bands, axis=0)
+    return jnp.concatenate(
+        [matrix[block_of(i), block_of(j)] for i in range(blocks) for j in range(i + 1)], axis=0
+    )
 
 
 def folded_blocks(blocks):
     for i in range(blocks):
-        band, begin = (i, 0) if i < blocks // 2 else (blocks - 1 - i, blocks - i)
         for j in range(i + 1):
-            yield i, j, band, begin + j
+            yield i, j, i * (i + 1) // 2 + j
 
 
 def block_of(i):
@@ -124,9 +119,9 @@
     row_index = lax.broadcasted_iota(jnp.int32, (BLOCK, BLOCK), 0)
     lane_index = lax.broadcasted_iota(jnp.int32, (BLOCK, BLOCK), 1)
     ridge = jnp.where(row_index == lane_index, ridge_term, 0.0)
-    for i, j, band, place in folded_blocks(size // BLOCK):
+    for i, j, place in folded_blocks(size // BLOCK):
         between = exact_dot(left_ref[:, block_of(i)], right_ref[:, block_of(j)], 0, 0)
-        block = (folded_ref[block_of(band), block_of(place)] + between) * scale
+        block = (folded_ref[block_of(place), :] + between) * scale
         if i == j:
             out_ref[block_of(i), block_of(i)] = block + ridge
         else:
@@ -177,7 +172,7 @@
         scratch_shapes=[pltpu.VMEM((6 * BLOCK, size), jnp.bfloat16)],
         compiler_params=pltpu.CompilerParams(vmem_limit_bytes=40 * 1024 * 1024),
         cost_estimate=pl.CostEstimate(
-            flops=120 * size * size * size, bytes_accessed=8 * size * size, transcendentals=0
+            flops=size * size * size, bytes_accessed=8 * size * size, transcendentals=0
         ),
         name="negative_inverse",
     )(folded, left, right, scale)
@@ -194,9 +189,9 @@
         for place, piece in enumerate(split3(block)):
             wide[place, rows, columns] = piece
 
-    for i, j, band, place in folded_blocks(size // BLOCK):
+    for i, j, place in folded_blocks(size // BLOCK):
         between = exact_dot(left_ref[:, block_of(i)], right_ref[:, block_of(j)], 0, 0)
-        block = (folded_ref[block_of(band), block_of(place)] + between) * scale
+        block = (folded_ref[block_of(place), :] + between) * scale
         put(lag_wide, block_of(i), block_of(j), block)
         if i != j:
             put(lag_wide, block_of(j), block_of(i), block.T)
@@ -264,6 +259,147 @@
     )(folded, left, right, scale, inverse, first, image, shifted)
 
 
+def routes(trajs, segs):
+    seg_bits = [("seg", 1 << i) for i in range(segs.bit_length() - 1)]
+    traj_bits = [("traj", 1 << i) for i in range(trajs.bit_length() - 1)]
+
+    def woven(first, second):
+        out = []
+        for i in range(max(len(first), len(second))):
+            out += first[i : i + 1] + second[i : i + 1]
+        return out
+
+    return (
+        seg_bits[:1] + woven(seg_bits[1:], traj_bits),
+        seg_bits[:1] + woven(traj_bits, seg_bits[1:]),
+    )
+
+
+def sum_kernel(trajs, segs, loads, outs, landings, send_sems, recv_sems):
+    traj, seg = lax.axis_index("traj"), lax.axis_index("seg")
+    core = seg % 2
+    devices = trajs * segs
+
+    def hop(axis, stride):
+        bit = ((seg if axis == "seg" else traj) // stride) % 2
+        move = stride * (1 - 2 * bit)
+        return bit, (move if axis == "traj" else 0 * move), (move if axis == "seg" else 0 * move)
+
+    def steps_of(stream):
+        steps = []
+        for one, other in zip(*routes(trajs, segs)):
+            if stream == 1:
+                one, other = other, one
+            bit, by_traj, by_seg = (
+                (1 - core) * a + core * b for a, b in zip(hop(*one), hop(*other))
+            )
+            steps.append((bit, (traj + by_traj, seg + by_seg)))
+        return steps
+
+    plans = [steps_of(stream) for stream in range(len(loads))]
+    count = len(plans[0])
+
+    barrier = pltpu.get_barrier_semaphore()
+    for _, partner in plans[0]:
+        pl.semaphore_signal(
+            barrier, inc=1, device_id=partner, device_id_type=pl.DeviceIdType.MESH
+        )
+    pl.semaphore_wait(barrier, count)
+
+    lows = [0 * traj for _ in loads]
+    kept = [[] for _ in loads]
+    flying = [None for _ in loads]
+
+    def send(stream, phase, source, target, partner):
+        place = stream * 2 * count + phase
+        flying[stream] = pltpu.make_async_remote_copy(
+            src_ref=source,
+            dst_ref=target,
+            send_sem=send_sems.at[place],
+            recv_sem=recv_sems.at[place],
+            device_id=partner,
+            device_id_type=pl.DeviceIdType.MESH,
+        )
+        flying[stream].start()
+
+    def held(stream, phase):
+        half = devices >> (phase + 1)
+        bit = plans[stream][phase][0]
+        if phase == 0:
+            return loads[stream], bit * half, (1 - bit) * half
+        begins = devices - 4 * half
+        return landings[stream], begins + bit * half, begins + (1 - bit) * half
+
+    def begin(stream, phase):
+        if phase < count:
+            half = devices >> (phase + 1)
+            source, _, give = held(stream, phase)
+            kept[stream].append(lows[stream] + plans[stream][phase][0] * half)
+            lows[stream] = kept[stream][-1]
+            send(
+                stream,
+                phase,
+                source.at[pl.ds(give, half)],
+                landings[stream].at[pl.ds(devices - 2 * half, half)],
+                plans[stream][phase][1],
+            )
+        else:
+            step = 2 * count - 1 - phase
+            span = outs[stream].at[pl.ds(kept[stream][step], devices >> (step + 1))]
+            send(stream, phase, span, span, plans[stream][step][1])
+
+    def end(stream, phase):
+        flying[stream].wait()
+        if phase < count:
+            half = devices >> (phase + 1)
+            source, keep, _ = held(stream, phase)
+            landed = devices - 2 * half
+            landing = landings[stream]
+            if phase == count - 1:
+                outs[stream][lows[stream]] = source[keep] + landing[landed]
+            else:
+
+                @pl.loop(0, half)
+                def _(i):
+                    landing[landed + i] = source[keep + i] + landing[landed + i]
+
+    for phase in range(2 * count + 1):
+        for stream in range(len(loads)):
+            if phase > 0:
+                end(stream, phase - 1)
+            if phase < 2 * count:
+                begin(stream, phase)
+
+
+def sum_over_devices(loads, trajs, segs):
+    steps = (trajs * segs).bit_length() - 1
+    number = len(loads)
+    vmem = pl.BlockSpec(memory_space=pltpu.VMEM)
+
+    def body(*refs):
+        groups = [refs[i * number : (i + 1) * number] for i in range(3)]
+        sum_kernel(trajs, segs, *groups, *refs[3 * number :])
+
+    return pl.pallas_call(
+        body,
+        out_shape=[jax.ShapeDtypeStruct(load.shape, jnp.float32) for load in loads],
+        in_specs=[vmem] * number,
+        out_specs=[vmem] * number,
+        scratch_shapes=[
+            *(pltpu.VMEM((trajs * segs - 1, *load.shape[1:]), jnp.float32) for load in loads),
+            pltpu.SemaphoreType.DMA((2 * steps * number,)),
+            pltpu.SemaphoreType.DMA((2 * steps * number,)),
+        ],
+        compiler_params=pltpu.CompilerParams(
+            collective_id=0, has_side_effects=True, vmem_limit_bytes=48 * 1024 * 1024
+        ),
+        cost_estimate=pl.CostEstimate(
+            flops=10**9, bytes_accessed=10**7, transcendentals=0
+        ),
+        name="sum_over_devices",
+    )(*loads)
+
+
 def featurize(frames, selection):
     frame_rows, parts, atoms = frames.shape
     offset = exact_dot(jnp.swapaxes(frames, 0, 1).reshape(parts * frame_rows, atoms), selection)
@@ -314,26 +450,27 @@
     )
     slot_length = jnp.pad(slot_length[None], ((0, 7), (0, feature_count - trajs)))
 
+    folded_rows = (feature_count // BLOCK) * (feature_count // BLOCK + 1) // 2 * BLOCK
+
     def load_of(gram, slots):
-        folded = fold(gram)
-        rows = folded.shape[0]
-        slots = jnp.concatenate(slots, axis=0)
-        wide = -(-slots.size // (rows * BLOCK)) * BLOCK
-        taken = wide * rows // feature_count
-        slots = jnp.pad(slots, ((0, taken - slots.shape[0]), (0, 0)))
-        return jnp.concatenate([folded, slots.reshape(rows, wide)], axis=1)
+        slots = jnp.concatenate(slots, axis=0).reshape(-1, BLOCK)
+        loaded = folded_rows + slots.shape[0]
+        share = -(-loaded // (8 * devices)) * 8
+        slots = jnp.pad(slots, ((0, share * devices - loaded), (0, 0)))
+        return jnp.concatenate([fold(gram), slots], axis=0).reshape(devices, share, BLOCK)
 
     def unload(total):
-        wide = feature_count + BLOCK
-        return total[:, :wide], total[:, wide:].reshape(-1, feature_count)
+        total = total.reshape(-1, BLOCK)
+        slots = total[folded_rows:]
+        per = feature_count // BLOCK
+        slots = slots[: slots.shape[0] // per * per]
+        return total, slots.reshape(-1, feature_count)
 
     first_load = load_of(gram_zero, [jnp.where(mine, own_all[None], 0.0), slot_length])
-    first_total = lax.psum(first_load, ("traj", "seg"))
     second_load = load_of(
         gram_lag, [jnp.where(mine, own_lead[None], 0.0), jnp.where(mine, own_ahead[None], 0.0)]
     )
-    second_load, first_total = lax.optimization_barrier((second_load, first_total))
-    second_total = lax.psum(second_load, ("traj", "seg"))
+    first_total, second_total = sum_over_devices((first_load, second_load), trajs, segs)
 
     folded_zero, slots = unload(first_total)
     all_lengths = slots[devices, :trajs]

time: 352 us -> 292 us (0.83)
  waiting for transfers between devices: 179 us -> 0.01 us
  Pallas kernels: 109 us -> 196 us
  local copies, waits for them, and re-layouts: 14.4 us -> 64.6 us
  between operations: 17.1 us -> 3.86 us
    psum x2 -> x0, waiting for transfers between devices: 179 us -> none  [the longest x1 127 us: on_device(): first_total = lax.psum(first_load, ('traj', 'seg'))]
    pallas_call x0 -> x1, Pallas kernels: none -> 86.6 us  [sum_over_devices(): pl.pallas_call(body, out_shape=[jax.ShapeDtypeStruct(load.shape, jnp.floa...]
    unnamed x12 -> x80, local copies, waits for them, and re-layouts: 3.48 us -> 57.5 us
    slice x19 -> x1, local copies, waits for them, and re-layouts: 6.91 us -> 0.02 us  [unload(): slots = total[folded_rows:]]
    concatenate x4 -> x2, other arithmetic: 4.47 us -> 0.03 us  [load_of(): slots = jnp.concatenate(slots, axis=0).reshape(-1, BLOCK)]
  transfers between devices with their start and end apart: 3 -> 1, of which waited for: 2 -> 0; matrix products, arithmetic and copies ran while one was open for 4% -> 2% of each run, Pallas kernels for 23% -> 0%
where the time goes in v1:
time: 292 us; the launch traced here: 290 us
  Pallas kernels  196 us (67%)
  local copies, waits for them, and re-layouts  64.6 us (22%)
  matrix products  15.6 us (5%)
  other arithmetic  7.63 us (3%)
  between operations  3.86 us (1%)
    pallas_call x1, Pallas kernels, sum_over_devices(): pl.pallas_call(body, out_shape=[jax.ShapeDtypeStruct(load.shape, jnp.floa...  86.6 us
    pallas_call x1, Pallas kernels, negative_inverse(): pl.pallas_call(lambda *refs: inverse_kernel(min(256, size), *refs), out_s...  79.2 us
    unnamed x80, local copies, waits for them, and re-layouts  57.5 us
    pallas_call x1, Pallas kernels, sweeps(): pl.pallas_call(lambda *refs: sweep_kernel(min(256, size), *refs), out_sha...  29.9 us
    dot_general x4, matrix products, exact_dot(): lax.dot_general(left, right, (((left_axis,), (right_axis,)), ((), ())), p...  15.6 us
  transfers between devices with their start and end apart: 1, of which 0 were waited for; matrix products, arithmetic and copies ran while one was open for 2% of the time, Pallas kernels for 0%

profile of v1, /device:TPU:9, one launch (start us, length us, event | category | flops | bytes accessed | tf_op | source)
XLA Modules:
  0.0 289.9 jit_solution(2502071883431849108)
XLA Ops:
  0.9 2.6 collective-permute-start
  4.3 4.3 %fusion.2 = f32[1024,384]{0,1:T(8,128)S(1)} fusion(f32[384,512]{1,0:T(8,128)} %bitcast.39, s32[1024]{0:T(1024)S(1)} %bitcast.42, s32[1024]{0:T(1024)S(1)} %bitcast.40), kind=kOutput, calls=%fused_computation.5 | convolution fusion | flops 2418933760 | bytes 2367488 | tf_op jit(solution)/shard_map/dot_general | solution.py:22
  11.6 1.8 fusion.4
  14.1 3.7 %fusion.5 = f32[1024,1024]{1,0:T(8,128)S(1)} fusion(f32[128,1024]{1,0:T(8,128)S(1)} %get-tuple-element.44, f32[128,1024]{1,0:T(8,128)S(1)} %get-tuple-element.43), kind=kOutput, calls=%fused_computation.8 | convolution fusion | flops 3221749760 | bytes 5242880 | tf_op jit(solution)/shard_map/dot_general | solution.py:22
  18.5 5.8 %fusion.16 = f32[1024,1024]{1,0:T(8,128)} fusion(f32[1024]{0:T(1024)S(1)} %broadcast_divide_fusion.5, f32[128]{0:T(128)S(1)} %get-tuple-element.46, f32[128,1024]{1,0:T(8,128)S(1)} %reduce_sum.108), kind=kOutput, calls=%fused_computation.25 | convolution fusion | flops 1611005952 | bytes 4723200 | tf_op jit(solution)/shard_map/dot_general | solution.py:22
  24.5 1.6 constant_dynamic-update-slice_fusion.34
  26.0 1.5 constant_dynamic-update-slice_fusion.33
  27.5 1.5 constant_dynamic-update-slice_fusion.32
  30.4 1.5 constant_dynamic-update-slice_fusion.30
  31.9 1.5 constant_dynamic-update-slice_fusion.29
  33.3 1.5 constant_dynamic-update-slice_fusion.28
  36.2 1.5 constant_dynamic-update-slice_fusion.26
  39.2 1.5 constant_dynamic-update-slice_fusion.24
  42.1 1.5 constant_dynamic-update-slice_fusion.22
  46.5 1.5 constant_dynamic-update-slice_fusion.19
  52.3 1.5 constant_dynamic-update-slice_fusion.15
  53.8 1.5 constant_dynamic-update-slice_fusion.14
  56.7 1.5 constant_dynamic-update-slice_fusion.12
  58.2 1.5 constant_dynamic-update-slice_fusion.11
  59.6 1.5 constant_dynamic-update-slice_fusion.10
  62.5 1.5 constant_dynamic-update-slice_fusion.8
  64.0 1.5 constant_dynamic-update-slice_fusion.7
  65.5 1.5 constant_dynamic-update-slice_fusion.6
  69.8 1.5 constant_dynamic-update-slice_fusion.3
  71.3 1.5 constant_dynamic-update-slice_fusion.2
  77.3 86.6 %sum_over_devices.1 = (f32[32,160,128]{2,1,0:T(8,128)S(1)}, f32[32,160,128]{2,1,0:T(8,128)S(1)}) custom-call(f32[32,160,128]{2,1,0:T(8,128)} %bitcast.8.refs_0_, f32[32,160,128]{2,1,0:T(8,128)} %bitcast.36), custom_call_target="tpu_custom_call" | custom-call | flops 1000000000 | bytes 10000000 | tf_op jit(solution)/shard_map/sum_over_devices/pallas_call | solution.py:383
  163.9 1.5 copy-done.1
  171.7 1.6 slice.337
  177.1 1.7 copy-done.2
  178.8 79.2 %negative_inverse.1 = (f32[1024,1024]{1,0:T(8,128)S(1)}, f32[128,128]{1,0:T(8,128)S(1)}, f32[1024,128]{1,0:T(8,128)S(1)}) custom-call(f32[5120,128]{1,0:T(8,128)S(1)} %bitcast.35, f32[32,1024]{1,0:T(8,128)S(1)} %get-tuple-element.22.refs_1_, f32[32,1024]{1,0:T(8,128)S(1)} %get-tuple-element.23.refs_2_, f32[1,1]{1,0:T(1,128)} %bitcast.17.refs_3_), custom_call_target="tpu_custom_call" | custom-call | flops 1073741824 | bytes 8388608 | tf_op jit(solution)/shard_map/negative_inverse/pallas_call | solution.py:163
  258.1 1.9 copy-done
  260.0 29.9 %sweeps.1 = f32[128,128]{1,0:T(8,128)} custom-call(f32[5120,128]{1,0:T(8,128)S(1)} %bitcast.32, f32[64,1024]{1,0:T(8,128)S(1)} %pad_maximum_fusion.2.refs_1_, f32[64,1024]{1,0:T(8,128)S(1)} %pad_maximum_fusion.3.refs_2_, f32[1,1]{1,0:T(1,128)} %bitcast.16.refs_3_, f32[1024,1024]{1,0:T(8,128)} %copy-done, f32[128,128]{1,0:T(8,128)S(1)} %get-tuple-element.13.refs_5_, ...), custom_call_target="tpu_custom_call" | custom-call | tf_op jit(solution)/shard_map/sweeps/pallas_call | solution.py:243
  (104 shorter events, 36.2 us)
Async XLA Ops:
  0.9 10.7 %collective-permute-start = (f32[10,3,512]{2,0,1:T(8,128)S(1)}, f32[10,3,512]{2,0,1:T(8,128)S(1)}, u32[]{:S(2)}, u32[]{:S(2)}) collective-permute-start(f32[10,3,512]{2,0,1:T(8,128)S(1)} %slice_bitcast_fusion), channel_id=1, source_target_pairs={{1,0},{2,1},{3,2},{5,4},{6,5},{7,6},{9,8},{10,9},{11,10},{13,12},{... | collective-permute-start | bytes 184328 | tf_op jit(solution)/shard_map/ppermute | solution.py:420
  8.7 9.8 %copy-start.3 = (f32[128,1024]{1,0:T(8,128)}, f32[128,1024]{1,0:T(8,128)S(1)}, u32[]{:S(2)}) copy-start(f32[128,1024]{1,0:T(8,128)S(1)} %reduce_sum.108) | copy-start | bytes 1572868
  75.8 1.6 copy-start.4
  163.9 1.5 copy-start.1
  177.1 1.7 copy-start.2
  258.1 1.9 copy-start

commit v2 on v1

--- a/solution.py
+++ b/solution.py
@@ -96,13 +96,6 @@
     return jnp.where(lane_index <= row_index, out, 0.0)
 
 
-def fold(matrix):
-    blocks = matrix.shape[0] // BLOCK
-    return jnp.concatenate(
-        [matrix[block_of(i), block_of(j)] for i in range(blocks) for j in range(i + 1)], axis=0
-    )
-
-
 def folded_blocks(blocks):
     for i in range(blocks):
         for j in range(i + 1):
@@ -259,6 +252,40 @@
     )(folded, left, right, scale, inverse, first, image, shifted)
 
 
+def gram_kernel(zero_ref, lead_ref, ahead_ref, zero_slots, lag_slots, zero_out, lag_out):
+    size = zero_ref.shape[1]
+    left = jnp.concatenate([lead_ref[...], ahead_ref[...]], axis=0)
+    right = jnp.concatenate([ahead_ref[...], lead_ref[...]], axis=0)
+    zero = zero_ref[...]
+    for i in range(size // BLOCK):
+        upto = (i + 1) * BLOCK
+        band_zero = exact_dot(zero[:, block_of(i)], zero[:, :upto], 0, 0)
+        band_lag = exact_dot(left[:, block_of(i)], right[:, :upto], 0, 0)
+        for j in range(i + 1):
+            place = block_of(i * (i + 1) // 2 + j)
+            zero_out[place, :] = band_zero[:, block_of(j)]
+            lag_out[place, :] = band_lag[:, block_of(j)]
+    for slots, out in ((zero_slots, zero_out), (lag_slots, lag_out)):
+        out[out.shape[0] - slots.shape[0] :, :] = slots[...]
+
+
+def grams(zero, lead, ahead, zero_slots, lag_slots):
+    blocks = zero.shape[1] // BLOCK
+    folded = blocks * (blocks + 1) // 2 * BLOCK
+    vmem = pl.BlockSpec(memory_space=pltpu.VMEM)
+    return pl.pallas_call(
+        gram_kernel,
+        out_shape=[
+            jax.ShapeDtypeStruct((folded + slots.shape[0], BLOCK), jnp.float32)
+            for slots in (zero_slots, lag_slots)
+        ],
+        in_specs=[vmem] * 5,
+        out_specs=[vmem] * 2,
+        compiler_params=pltpu.CompilerParams(vmem_limit_bytes=40 * 1024 * 1024),
+        name="grams",
+    )(zero, lead, ahead, zero_slots, lag_slots)
+
+
 def routes(trajs, segs):
     seg_bits = [("seg", 1 << i) for i in range(segs.bit_length() - 1)]
     traj_bits = [("traj", 1 << i) for i in range(trajs.bit_length() - 1)]
@@ -436,14 +463,6 @@
     centered = (features - own_all) * is_valid
     lead_rows = (features - own_lead) * paired
     ahead_rows = (lagged - own_ahead) * paired
-    gram_zero = exact_dot(centered, centered, 0, 0)
-    gram_lag = exact_dot(
-        jnp.concatenate([lead_rows, ahead_rows], axis=0),
-        jnp.concatenate([ahead_rows, lead_rows], axis=0),
-        0,
-        0,
-    )
-
     mine = (jnp.arange(devices) == me)[:, None]
     slot_length = jnp.where(
         (jnp.arange(trajs) == traj) & (seg == 0), length.astype(jnp.float32), 0.0
@@ -452,12 +471,11 @@
 
     folded_rows = (feature_count // BLOCK) * (feature_count // BLOCK + 1) // 2 * BLOCK
 
-    def load_of(gram, slots):
+    def padded(slots):
         slots = jnp.concatenate(slots, axis=0).reshape(-1, BLOCK)
         loaded = folded_rows + slots.shape[0]
         share = -(-loaded // (8 * devices)) * 8
-        slots = jnp.pad(slots, ((0, share * devices - loaded), (0, 0)))
-        return jnp.concatenate([fold(gram), slots], axis=0).reshape(devices, share, BLOCK)
+        return jnp.pad(slots, ((0, share * devices - loaded), (0, 0)))
 
     def unload(total):
         total = total.reshape(-1, BLOCK)
@@ -466,11 +484,17 @@
         slots = slots[: slots.shape[0] // per * per]
         return total, slots.reshape(-1, feature_count)
 
-    first_load = load_of(gram_zero, [jnp.where(mine, own_all[None], 0.0), slot_length])
-    second_load = load_of(
-        gram_lag, [jnp.where(mine, own_lead[None], 0.0), jnp.where(mine, own_ahead[None], 0.0)]
-    )
-    first_total, second_total = sum_over_devices((first_load, second_load), trajs, segs)
+    loads = grams(
+        centered,
+        lead_rows,
+        ahead_rows,
+        padded([jnp.where(mine, own_all[None], 0.0), slot_length]),
+        padded(
+            [jnp.where(mine, own_lead[None], 0.0), jnp.where(mine, own_ahead[None], 0.0)]
+        ),
+    )
+    loads = [load.reshape(devices, -1, BLOCK) for load in loads]
+    first_total, second_total = sum_over_devices(loads, trajs, segs)
 
     folded_zero, slots = unload(first_total)
     all_lengths = slots[devices, :trajs]

time: 292 us -> 235 us (0.80)
  local copies, waits for them, and re-layouts: 64.6 us -> 14.4 us
  matrix products: 15.6 us -> 6.08 us
  Pallas kernels: 196 us -> 200 us
    unnamed x80 -> x12, local copies, waits for them, and re-layouts: 57.5 us -> 8.18 us
    dot_general x4 -> x2, matrix products: 15.6 us -> 6.08 us  [exact_dot(): lax.dot_general(left, right, (((left_axis,), (right_axis,)), ((), ())), p...]
    pallas_call x0 -> x1, Pallas kernels: none -> 4.16 us  [grams(): pl.pallas_call(gram_kernel, out_shape=[jax.ShapeDtypeStruct((folded + slo...]
  transfers between devices with their start and end apart: 1 -> 1, of which waited for: 0 -> 0; matrix products, arithmetic and copies ran while one was open for 2% -> 3% of each run, Pallas kernels for 0% -> 0%
where the time goes in v2:
time: 235 us; the launch traced here: 234 us
  Pallas kernels  200 us (85%)
  local copies, waits for them, and re-layouts  14.4 us (6%)
  other arithmetic  7.71 us (3%)
  matrix products  6.08 us (3%)
  between operations  3.57 us (2%)
  starting transfers between devices  2.57 us (1%)
    pallas_call x1, Pallas kernels, sum_over_devices(): pl.pallas_call(body, out_shape=[jax.ShapeDtypeStruct(load.shape, jnp.floa...  86.5 us
    pallas_call x1, Pallas kernels, negative_inverse(): pl.pallas_call(lambda *refs: inverse_kernel(min(256, size), *refs), out_s...  79 us
    pallas_call x1, Pallas kernels, sweeps(): pl.pallas_call(lambda *refs: sweep_kernel(min(256, size), *refs), out_sha...  30.1 us
    unnamed x12, local copies, waits for them, and re-layouts  8.18 us
    dot_general x2, matrix products, exact_dot(): lax.dot_general(left, right, (((left_axis,), (right_axis,)), ((), ())), p...  6.08 us
  transfers between devices with their start and end apart: 1, of which 0 were waited for; matrix products, arithmetic and copies ran while one was open for 3% of the time, Pallas kernels for 0%

profile of v2, /device:TPU:9, one launch (start us, length us, event | category | flops | bytes accessed | tf_op | source)
XLA Modules:
  0.0 234.1 jit_solution(658992612215139371)
XLA Ops:
  0.0 0.9 slice_bitcast_fusion
  0.9 2.6 %collective-permute-start = (f32[10,3,512]{2,0,1:T(8,128)S(1)}, f32[10,3,512]{2,0,1:T(8,128)S(1)}, u32[]{:S(2)}, u32[]{:S(2)}) collective-permute-start(f32[10,3,512]{2,0,1:T(8,128)S(1)} %slice_bitcast_fusion), channel_id=1, source_target_pairs={{1,0},{2,1},{3,2},{5,4},{6,5},{7,6},{9,8},{10,9},{11,10},{13,12},{... | collective-permute-start | bytes 184328 | tf_op jit(solution)/shard_map/ppermute | solution.py:447
  4.1 0.8 fusion.14
  4.9 4.3 %fusion.2 = f32[1024,384]{0,1:T(8,128)S(1)} fusion(f32[384,512]{1,0:T(8,128)} %bitcast.40, s32[1024]{0:T(1024)S(1)} %bitcast.43, s32[1024]{0:T(1024)S(1)} %bitcast.41), kind=kOutput, calls=%fused_computation.5 | convolution fusion | flops 2418933760 | bytes 2367488 | tf_op jit(solution)/shard_map/dot_general | solution.py:22
  9.2 0.1 reduce_sum.108
  9.4 0.1 add_sqrt_fusion
  9.6 0.7 fusion.11
  11.6 1.8 fusion.4
  13.5 0.3 multiply_reduce_fusion.1
  13.9 0.3 subtract_multiply_fusion.2
  14.2 0.1 broadcast_select_fusion.1
  14.5 4.2 %grams.1 = (f32[5120,128]{1,0:T(8,128)S(1)}, f32[5120,128]{1,0:T(8,128)S(1)}) custom-call(f32[128,1024]{1,0:T(8,128)S(1)} %get-tuple-element.39.zero_ref, f32[128,1024]{1,0:T(8,128)S(1)} %get-tuple-element.38.lead_ref, f32[128,1024]{1,0:T(8,128)S(1)} %get-tuple-element.49.ahead_ref, f32[512,128]{1,0:T(8,128)S(1)} %pad.9.zero_slots, ...), custom_call_target="tpu_custom_call" | custom-call | tf_op jit(solution)/shard_map/grams/pallas_call | solution.py:276
  18.6 1.5 copy-done.1
  20.1 1.5 copy-done.2
  21.7 86.5 %sum_over_devices.1 = (f32[32,160,128]{2,1,0:T(8,128)S(1)}, f32[32,160,128]{2,1,0:T(8,128)S(1)}) custom-call(f32[32,160,128]{2,1,0:T(8,128)} %bitcast.33, f32[32,160,128]{2,1,0:T(8,128)} %bitcast.34), custom_call_target="tpu_custom_call" | custom-call | flops 1000000000 | bytes 10000000 | tf_op jit(solution)/shard_map/sum_over_devices/pallas_call | solution.py:410
  108.2 1.5 copy-done.3
  109.8 0.9 slice.61
  110.7 0.7 fusion.10
  112.2 0.1 multiply_reduce_fusion.3
  112.3 0.7 broadcast_divide_fusion
  113.0 1.2 subtract_multiply_fusion.refs_7_
  114.3 0.7 fusion.13
  115.0 0.9 slice.49
  116.0 1.6 slice.53
  117.5 1.0 multiply_reduce_fusion.5
  118.5 0.6 broadcast_divide_fusion.1
  119.1 0.6 broadcast_divide_fusion.2
  120.3 1.0 broadcast_multiply_fusion.2
  121.3 1.7 copy-done.4
  123.1 79.0 %negative_inverse.1 = (f32[1024,1024]{1,0:T(8,128)S(1)}, f32[128,128]{1,0:T(8,128)S(1)}, f32[1024,128]{1,0:T(8,128)S(1)}) custom-call(f32[5120,128]{1,0:T(8,128)S(1)} %bitcast.37, f32[32,1024]{1,0:T(8,128)S(1)} %get-tuple-element.26.refs_1_, f32[32,1024]{1,0:T(8,128)S(1)} %get-tuple-element.27.refs_2_, f32[1,1]{1,0:T(1,128)} %bitcast.17.refs_3_), custom_call_target="tpu_custom_call" | custom-call | flops 1073741824 | bytes 8388608 | tf_op jit(solution)/shard_map/negative_inverse/pallas_call | solution.py:156
  202.1 1.9 copy-done
  204.0 30.1 %sweeps.1 = f32[128,128]{1,0:T(8,128)} custom-call(f32[5120,128]{1,0:T(8,128)S(1)} %bitcast.32, f32[64,1024]{1,0:T(8,128)S(1)} %pad_maximum_fusion.2.refs_1_, f32[64,1024]{1,0:T(8,128)S(1)} %pad_maximum_fusion.3.refs_2_, f32[1,1]{1,0:T(1,128)} %bitcast.16.refs_3_, f32[1024,1024]{1,0:T(8,128)} %copy-done, f32[128,128]{1,0:T(8,128)S(1)} %get-tuple-element.17.refs_5_, ...), custom_call_target="tpu_custom_call" | custom-call | tf_op jit(solution)/shard_map/sweeps/pallas_call | solution.py:236
  (34 shorter events, 0.7 us)
Async XLA Ops:
  0.9 10.7 %collective-permute-start = (f32[10,3,512]{2,0,1:T(8,128)S(1)}, f32[10,3,512]{2,0,1:T(8,128)S(1)}, u32[]{:S(2)}, u32[]{:S(2)}) collective-permute-start(f32[10,3,512]{2,0,1:T(8,128)S(1)} %slice_bitcast_fusion), channel_id=1, source_target_pairs={{1,0},{2,1},{3,2},{5,4},{6,5},{7,6},{9,8},{10,9},{11,10},{13,12},{... | collective-permute-start | bytes 184328 | tf_op jit(solution)/shard_map/ppermute | solution.py:447
  9.4 4.5 %copy-start.5 = (f32[128,1024]{1,0:T(8,128)}, f32[128,1024]{1,0:T(8,128)S(1)}, u32[]{:S(2)}) copy-start(f32[128,1024]{1,0:T(8,128)S(1)} %reduce_sum.108) | copy-start | bytes 1572868
  18.6 1.5 copy-start.1
  20.1 1.5 copy-start.2
  108.2 1.5 copy-start.3
  121.3 1.7 copy-start.4
  202.1 1.9 copy-start

commit v3 on v2

--- a/solution.py
+++ b/solution.py
@@ -106,7 +106,7 @@
     return slice(i * BLOCK, (i + 1) * BLOCK)
 
 
-def inverse_kernel(tile, folded_ref, left_ref, right_ref, scale_ref, out_ref, first_ref, image_ref, wide):
+def inverse_kernel(tile, folded_ref, left_ref, right_ref, scale_ref, out_ref, first_ref, image_ref, wide, held):
     size = out_ref.shape[0]
     scale = scale_ref[0, 0]
     row_index = lax.broadcasted_iota(jnp.int32, (BLOCK, BLOCK), 0)
@@ -121,31 +121,37 @@
             out_ref[block_of(i), block_of(j)] = block
             out_ref[block_of(j), block_of(i)] = block.T
 
+    first = inverse_factor(out_ref[:BLOCK, :BLOCK])
+    first_ref[...] = first
+    held[...] = first
+    image_ref[...] = exact_dot(out_ref[:, :BLOCK], first, 1, 1)
+    last = size // BLOCK - 1
+
+    def long_of(column):
+        h, m, l = split3(column)
+        return jnp.concatenate([h, h, m, m, h, l], axis=1)
+
     @pl.loop(0, size // BLOCK)
     def _(k):
         here = pl.ds(pl.multiple_of(k * BLOCK, BLOCK), BLOCK)
-        factor = inverse_factor(out_ref[here, here])
-
-        @pl.when(k == 0)
-        def _():
-            first_ref[...] = factor
-            image_ref[...] = exact_dot(out_ref[:, :BLOCK], factor, 1, 1)
-
+        then = pl.ds(pl.multiple_of(jnp.minimum(k + 1, last) * BLOCK, BLOCK), BLOCK)
+        factor = held[...]
         pivot = exact_dot(factor, factor, 0, 0)
         row = exact_dot(pivot, out_ref[here, :])
         high, middle, low = split3(row)
         for place, piece in enumerate((high, middle, high, middle, low, high)):
             wide[place * BLOCK : (place + 1) * BLOCK, :] = piece
-
-        @pl.loop(0, size // tile)
-        def _(i):
-            span = pl.ds(pl.multiple_of(i * tile, tile), tile)
+        ahead = out_ref[then, then] - jnp.dot(
+            long_of(out_ref[then, here]), wide[:, then], preferred_element_type=jnp.float32
+        )
+        held[...] = inverse_factor(ahead)
+        for i in range(size // tile):
+            span = slice(i * tile, (i + 1) * tile)
             column = out_ref[span, here]
-            h, m, l = split3(column)
-            long = jnp.concatenate([h, h, m, m, h, l], axis=1)
-            out_ref[span, :] -= jnp.dot(long, wide[...], preferred_element_type=jnp.float32)
+            out_ref[span, :] -= jnp.dot(
+                long_of(column), wide[...], preferred_element_type=jnp.float32
+            )
             out_ref[span, here] = exact_dot(column, pivot)
-
         out_ref[here, :] = row
         out_ref[here, here] = -pivot
 
@@ -162,7 +168,10 @@
         ),
         in_specs=[vmem, vmem, vmem, smem],
         out_specs=(vmem, vmem, vmem),
-        scratch_shapes=[pltpu.VMEM((6 * BLOCK, size), jnp.bfloat16)],
+        scratch_shapes=[
+            pltpu.VMEM((6 * BLOCK, size), jnp.bfloat16),
+            pltpu.VMEM((BLOCK, BLOCK), jnp.float32),
+        ],
         compiler_params=pltpu.CompilerParams(vmem_limit_bytes=40 * 1024 * 1024),
         cost_estimate=pl.CostEstimate(
             flops=size * size * size, bytes_accessed=8 * size * size, transcendentals=0

time: 235 us -> 223 us (0.949)
  Pallas kernels: 200 us -> 188 us
    pallas_call x1, Pallas kernels: 79 us -> 67.1 us  [negative_inverse(): pl.pallas_call(lambda *refs: inverse_kernel(min(256, size), *refs), out_s...]
where the time goes in v3:
time: 223 us; the launch traced here: 222 us
  Pallas kernels  188 us (84%)
  local copies, waits for them, and re-layouts  14.4 us (6%)
  other arithmetic  7.71 us (3%)
  matrix products  6.08 us (3%)
  between operations  3.57 us (2%)
  starting transfers between devices  2.57 us (1%)
    pallas_call x1, Pallas kernels, sum_over_devices(): pl.pallas_call(body, out_shape=[jax.ShapeDtypeStruct(load.shape, jnp.floa...  86.5 us
    pallas_call x1, Pallas kernels, negative_inverse(): pl.pallas_call(lambda *refs: inverse_kernel(min(256, size), *refs), out_s...  67.1 us
    pallas_call x1, Pallas kernels, sweeps(): pl.pallas_call(lambda *refs: sweep_kernel(min(256, size), *refs), out_sha...  30.1 us
    unnamed x12, local copies, waits for them, and re-layouts  8.18 us
    dot_general x2, matrix products, exact_dot(): lax.dot_general(left, right, (((left_axis,), (right_axis,)), ((), ())), p...  6.08 us
  transfers between devices with their start and end apart: 1, of which 0 were waited for; matrix products, arithmetic and copies ran while one was open for 3% of the time, Pallas kernels for 0%

profile of v3, /device:TPU:9, one launch (start us, length us, event | category | flops | bytes accessed | tf_op | source)
XLA Modules:
  0.0 222.2 jit_solution(15427740350552469808)
XLA Ops:
  0.0 0.9 slice_bitcast_fusion
  0.9 2.6 %collective-permute-start = (f32[10,3,512]{2,0,1:T(8,128)S(1)}, f32[10,3,512]{2,0,1:T(8,128)S(1)}, u32[]{:S(2)}, u32[]{:S(2)}) collective-permute-start(f32[10,3,512]{2,0,1:T(8,128)S(1)} %slice_bitcast_fusion), channel_id=1, source_target_pairs={{1,0},{2,1},{3,2},{5,4},{6,5},{7,6},{9,8},{10,9},{11,10},{13,12},{... | collective-permute-start | bytes 184328 | tf_op jit(solution)/shard_map/ppermute | solution.py:456
  4.1 0.8 fusion.14
  4.9 4.3 %fusion.2 = f32[1024,384]{0,1:T(8,128)S(1)} fusion(f32[384,512]{1,0:T(8,128)} %bitcast.40, s32[1024]{0:T(1024)S(1)} %bitcast.43, s32[1024]{0:T(1024)S(1)} %bitcast.41), kind=kOutput, calls=%fused_computation.5 | convolution fusion | flops 2418933760 | bytes 2367488 | tf_op jit(solution)/shard_map/dot_general | solution.py:22
  9.2 0.1 reduce_sum.108
  9.4 0.1 add_sqrt_fusion
  9.6 0.7 fusion.11
  11.6 1.8 fusion.4
  13.5 0.3 multiply_reduce_fusion.1
  13.9 0.3 subtract_multiply_fusion.2
  14.2 0.1 broadcast_select_fusion.1
  14.5 4.2 %grams.1 = (f32[5120,128]{1,0:T(8,128)S(1)}, f32[5120,128]{1,0:T(8,128)S(1)}) custom-call(f32[128,1024]{1,0:T(8,128)S(1)} %get-tuple-element.39.zero_ref, f32[128,1024]{1,0:T(8,128)S(1)} %get-tuple-element.38.lead_ref, f32[128,1024]{1,0:T(8,128)S(1)} %get-tuple-element.49.ahead_ref, f32[512,128]{1,0:T(8,128)S(1)} %pad.9.zero_slots, ...), custom_call_target="tpu_custom_call" | custom-call | tf_op jit(solution)/shard_map/grams/pallas_call | solution.py:285
  18.6 1.5 copy-done.1
  20.1 1.5 copy-done.2
  21.7 86.5 %sum_over_devices.1 = (f32[32,160,128]{2,1,0:T(8,128)S(1)}, f32[32,160,128]{2,1,0:T(8,128)S(1)}) custom-call(f32[32,160,128]{2,1,0:T(8,128)} %bitcast.33, f32[32,160,128]{2,1,0:T(8,128)} %bitcast.34), custom_call_target="tpu_custom_call" | custom-call | flops 1000000000 | bytes 10000000 | tf_op jit(solution)/shard_map/sum_over_devices/pallas_call | solution.py:419
  108.2 1.5 copy-done.3
  109.8 0.9 slice.61
  110.7 0.7 fusion.10
  112.2 0.1 multiply_reduce_fusion.3
  112.3 0.7 broadcast_divide_fusion
  113.0 1.2 subtract_multiply_fusion.refs_7_
  114.3 0.7 fusion.13
  115.0 0.9 slice.49
  116.0 1.6 slice.53
  117.5 1.0 multiply_reduce_fusion.5
  118.5 0.6 broadcast_divide_fusion.1
  119.1 0.6 broadcast_divide_fusion.2
  120.3 1.0 broadcast_multiply_fusion.2
  121.3 1.7 copy-done.4
  123.1 67.1 %negative_inverse.1 = (f32[1024,1024]{1,0:T(8,128)S(1)}, f32[128,128]{1,0:T(8,128)S(1)}, f32[1024,128]{1,0:T(8,128)S(1)}) custom-call(f32[5120,128]{1,0:T(8,128)S(1)} %bitcast.37, f32[32,1024]{1,0:T(8,128)S(1)} %get-tuple-element.26.refs_1_, f32[32,1024]{1,0:T(8,128)S(1)} %get-tuple-element.27.refs_2_, f32[1,1]{1,0:T(1,128)} %bitcast.17.refs_3_), custom_call_target="tpu_custom_call" | custom-call | flops 1073741824 | bytes 8388608 | tf_op jit(solution)/shard_map/negative_inverse/pallas_call | solution.py:162
  190.2 1.9 copy-done
  192.1 30.1 %sweeps.1 = f32[128,128]{1,0:T(8,128)} custom-call(f32[5120,128]{1,0:T(8,128)S(1)} %bitcast.32, f32[64,1024]{1,0:T(8,128)S(1)} %pad_maximum_fusion.2.refs_1_, f32[64,1024]{1,0:T(8,128)S(1)} %pad_maximum_fusion.3.refs_2_, f32[1,1]{1,0:T(1,128)} %bitcast.16.refs_3_, f32[1024,1024]{1,0:T(8,128)} %copy-done, f32[128,128]{1,0:T(8,128)S(1)} %get-tuple-element.17.refs_5_, ...), custom_call_target="tpu_custom_call" | custom-call | tf_op jit(solution)/shard_map/sweeps/pallas_call | solution.py:245
  (34 shorter events, 0.7 us)
Async XLA Ops:
  0.9 10.7 %collective-permute-start = (f32[10,3,512]{2,0,1:T(8,128)S(1)}, f32[10,3,512]{2,0,1:T(8,128)S(1)}, u32[]{:S(2)}, u32[]{:S(2)}) collective-permute-start(f32[10,3,512]{2,0,1:T(8,128)S(1)} %slice_bitcast_fusion), channel_id=1, source_target_pairs={{1,0},{2,1},{3,2},{5,4},{6,5},{7,6},{9,8},{10,9},{11,10},{13,12},{... | collective-permute-start | bytes 184328 | tf_op jit(solution)/shard_map/ppermute | solution.py:456
  9.4 4.5 %copy-start.5 = (f32[128,1024]{1,0:T(8,128)}, f32[128,1024]{1,0:T(8,128)S(1)}, u32[]{:S(2)}) copy-start(f32[128,1024]{1,0:T(8,128)S(1)} %reduce_sum.108) | copy-start | bytes 1572868
  18.6 1.5 copy-start.1
  20.1 1.5 copy-start.2
  108.2 1.5 copy-start.3
  121.3 1.7 copy-start.4
  190.2 1.9 copy-start
